TPU v7x, 1024 devices: a whole 8x8x8 slice. The times are simulated.
1024 devices in a mesh: dp: 16 (over z, core), expert: 64 (over x, y).
Axes of the slice: x: 8, y: 8, z: 8, core: 2. Of those that a mesh axis runs over, the one named last changes fastest.
Arguments:
- expert_inputs: bfloat16 [16, 64, 240, 2048], P('dp', 'expert'), may hold values from -6 to 6
- up_cotangent: bfloat16 [16, 64, 240, 768], P('dp', 'expert'), may hold values from -0.375 to 0.375
- row_counts: int32 [16, 64], P('dp', 'expert'), may hold values from 60 to 240, as said below
- weights: bfloat16 [2048, 64, 768], P('dp', 'expert'), may hold values from -6 to 6
- first_moment: bfloat16 [2048, 64, 768], P('dp', 'expert'), may hold values from -6 to 6
- second_moment: bfloat16 [2048, 64, 768], P('dp', 'expert'), may hold values from 0.049804688 to 2
- old_expert: int32 [64], replicated, may hold values from 0 to 63, each once
- new_expert: int32 [128], replicated, may hold values from 0 to 63, as said below
- slot_counts: int32 [64], replicated, may hold values from 1 to 2, as said below
Outputs:
- new_weights: bfloat16 [2048, 128, 768], P('dp', 'expert')
- new_first: bfloat16 [2048, 128, 768], P('dp', 'expert')
- new_second: bfloat16 [2048, 128, 768], P('dp', 'expert')
Inputs may be any that keep to these rules, and one draw needn't show every extreme that they name: `row_counts`: some replica of some expert has exactly 240 rows in every draw. `new_expert`: every expert is named by at least one live new slot; the live slots of one device name different experts; entries of slots that are not live are arbitrary expert numbers. `slot_counts`: every device keeps at least one expert; in every draw some device has 2 live slots and some other device one.
All inputs are finite; a program needn't handle non-finite values.
Results may differ from a plain program's by a relative error of at most 0.012.
Values may be sent and summed in bfloat16 or wider, within the bound.
A program may use at most 32 MiB of HBM per device.

v0:
```python
import jax
import jax.numpy as jnp
from jax import lax
from jax.sharding import PartitionSpec as P

beta_one = 0.9
beta_two = 0.95
learn_rate = 0.05
decay_rate = 0.1
epsilon = 1e-08
correct_one = 0.9999734386011124
correct_two = 0.994079470779666


def adamw_step(gradient, weight, first, second):
    first_new = beta_one * first.astype(jnp.float32) + (1.0 - beta_one) * gradient
    second_new = beta_two * second.astype(jnp.float32) + (1.0 - beta_two) * gradient * gradient
    direction = first_new / correct_one / (jnp.sqrt(second_new / correct_two) + epsilon)
    weight_full = weight.astype(jnp.float32)
    weight_new = weight_full - learn_rate * (direction + decay_rate * weight_full)
    return (
        weight_new.astype(jnp.bfloat16),
        first_new.astype(jnp.bfloat16),
        second_new.astype(jnp.bfloat16),
    )


def spread(state):
    return (
        lax.all_to_all(state[0], "expert", split_axis=2, concat_axis=1, tiled=True),
        lax.all_to_all(state[1], "expert", split_axis=2, concat_axis=1, tiled=True),
        lax.all_to_all(state[2], "expert", split_axis=2, concat_axis=1, tiled=True),
    )


def collect(state):
    return (
        lax.all_to_all(state[0], "expert", split_axis=1, concat_axis=2, tiled=True),
        lax.all_to_all(state[1], "expert", split_axis=1, concat_axis=2, tiled=True),
        lax.all_to_all(state[2], "expert", split_axis=1, concat_axis=2, tiled=True),
    )


def shards(
    expert_inputs,
    up_cotangent,
    row_counts,
    weights,
    first_moment,
    second_moment,
    old_expert,
    new_expert,
    slot_counts,
):
    inputs = expert_inputs[0, 0]
    cotangent = up_cotangent[0, 0]
    token_rows = inputs.shape[0]
    live_rows = jnp.arange(token_rows, dtype=jnp.int32)[:, None] < row_counts[0, 0]
    masked = jnp.where(live_rows, cotangent, jnp.zeros_like(cotangent))
    gradient = lax.psum_scatter(
        lax.dot_general(
            inputs, masked, (((0,), (0,)), ((), ())), preferred_element_type=jnp.float32
        ).astype(jnp.bfloat16),
        "dp",
        scatter_dimension=0,
        tiled=True,
    ).astype(jnp.float32)
    gradient = gradient[:, None, :]
    experts = old_expert.shape[0]
    slots_all = new_expert.shape[0]
    per_device = slots_all // experts
    matches = old_expert[None, :] == new_expert[:, None]
    source = jnp.sum(jnp.where(matches, jnp.arange(experts, dtype=jnp.int32)[None, :], 0), axis=1)
    keep_slot = jnp.arange(slots_all, dtype=jnp.int32) % per_device < jnp.repeat(
        slot_counts, per_device, total_repeat_length=slots_all
    )

    def choose_slots(table):
        chosen = jnp.take(table, source, axis=1)
        return jnp.where(keep_slot[None, :, None], chosen, jnp.zeros_like(chosen))

    updated = adamw_step(gradient, weights, first_moment, second_moment)
    middle = spread(updated)
    placed = (choose_slots(middle[0]), choose_slots(middle[1]), choose_slots(middle[2]))
    new_weights, new_first, new_second = collect(placed)
    return (new_weights, new_first, new_second)


def solution(mesh):
    return jax.shard_map(
        shards,
        mesh=mesh,
        in_specs=(
            P("dp", "expert", None, None),
            P("dp", "expert", None, None),
            P("dp", "expert"),
            P("dp", "expert", None),
            P("dp", "expert", None),
            P("dp", "expert", None),
            P(),
            P(),
            P(),
        ),
        out_specs=(P("dp", "expert", None), P("dp", "expert", None), P("dp", "expert", None)),
        check_vma=False,
    )
```

profile of v0, /device:TPU:260, one launch (start us, length us, event | category | flops | bytes accessed | tf_op | source)
XLA Modules:
  0.0 238.7 jit_solution(15003234959740818097)
XLA Ops:
  7.2 0.0 copy-start
  7.2 0.0 reduce-scatter.4.cloned.1.call-start
  8.0 0.4 copy-done
  8.4 3.8 %fusion = bf16[2048,768]{0,1:T(8,128)(2,1)} fusion(bf16[1,1,240,2048]{3,2,1,0:T(8,128)(2,1)S(1)} %copy-done, bf16[1,1,240,768]{3,2,1,0:T(8,128)(2,1)} %param.14, pred[240]{0:T(512)(128)(4,1)S(1)} %iota_compare_fusion), kind=kOutput, calls=%fused_computation.5 | convolution fusion | flops 756731904 | bytes 4497648 | tf_op jit(solution)/shard_map/dot_general | solution.py:61
  12.2 4.6 %copy.51 = bf16[2048,768]{1,0:T(8,128)(2,1)} copy(bf16[2048,768]{0,1:T(8,128)(2,1)} %fusion) | data formatting | bytes 6291456
  16.8 0.0 copy-start.2
  16.8 0.0 copy-start.3
  16.8 0.0 copy-start.4
  16.8 0.0 reduce-scatter.4.cloned.1.call-update
  16.9 0.9 copy-done.2
  17.8 0.0 copy-start.5
  17.8 0.0 copy-start.1
  17.8 0.0 copy-start.6
  17.8 0.0 copy-start.7
  17.8 0.2 copy.39
  17.9 0.0 copy-done.3
  17.9 0.2 copy.40
  18.1 0.0 copy-done.4
  18.1 0.2 copy.41
  18.3 68.3 %reduce-scatter.4.cloned.1.call-done = bf16[128,768]{1,0:T(8,128)(2,1)} async-done(((bf16[2048,768]{1,0:T(8,128)(2,1)}), bf16[128,768]{1,0:T(8,128)(2,1)}) %reduce-scatter.4.cloned.1.call-update) | async-done | bytes 196624
  86.6 1.1 copy.52
  87.7 0.4 fusion.12
  88.1 0.3 copy.61
  88.4 0.5 broadcast.142
  89.0 1.8 reduce.10
  90.8 0.8 reshape.132
  91.6 12.8 %all-to-all-start = ((bf16[64,2,768]{2,1,0:T(2,128)(2,1)}), bf16[64,2,768]{2,1,0:T(2,128)(2,1)S(1)}, u32[]{:S(2)}, u32[]{:S(2)}) async-start(bf16[64,2,768]{2,1,0:T(2,128)(2,1)} %reshape.132), calls=%async_computation | async-start | bytes 393216 | tf_op jit(solution)/shard_map/all_to_all | solution.py:30
  104.4 0.0 copy-done.5
  104.4 0.0 copy-done.1
  104.4 1.2 gather_fusion
  105.6 0.0 copy-done.6
  105.6 0.0 copy-done.7
  105.6 0.1 select_reduce_fusion
  105.7 0.3 copy.60
  106.1 1.9 reduce.9
  107.9 0.8 reshape.134
  108.7 7.4 %all-to-all-done = bf16[64,2,768]{2,1,0:T(2,128)(2,1)S(1)} async-done(((bf16[64,2,768]{2,1,0:T(2,128)(2,1)}), bf16[64,2,768]{2,1,0:T(2,128)(2,1)S(1)}, u32[]{:S(2)}, u32[]{:S(2)}) %all-to-all-start) | async-done | bytes 196640 | tf_op jit(solution)/shard_map/all_to_all | solution.py:30
  116.1 5.9 %all-to-all-start.2 = ((bf16[64,2,768]{2,1,0:T(2,128)(2,1)}), bf16[64,2,768]{2,1,0:T(2,128)(2,1)S(1)}, u32[]{:S(2)}, u32[]{:S(2)}) async-start(bf16[64,2,768]{2,1,0:T(2,128)(2,1)} %reshape.134), calls=%async_computation.2 | async-start | bytes 393216 | tf_op jit(solution)/shard_map/all_to_all | solution.py:31
  122.0 0.3 copy.59
  122.3 1.8 reduce.8
  124.2 0.8 reshape.136
  124.9 9.7 %all-to-all-done.2 = bf16[64,2,768]{2,1,0:T(2,128)(2,1)S(1)} async-done(((bf16[64,2,768]{2,1,0:T(2,128)(2,1)}), bf16[64,2,768]{2,1,0:T(2,128)(2,1)S(1)}, u32[]{:S(2)}, u32[]{:S(2)}) %all-to-all-start.2) | async-done | bytes 196640 | tf_op jit(solution)/shard_map/all_to_all | solution.py:31
  134.6 5.9 %all-to-all-start.4 = ((bf16[64,2,768]{2,1,0:T(2,128)(2,1)}), bf16[64,2,768]{2,1,0:T(2,128)(2,1)S(1)}, u32[]{:S(2)}, u32[]{:S(2)}) async-start(bf16[64,2,768]{2,1,0:T(2,128)(2,1)} %reshape.136), calls=%async_computation.4 | async-start | bytes 393216 | tf_op jit(solution)/shard_map/all_to_all | solution.py:32
  140.6 0.1 reshape.133
  140.7 1.1 bitcast_reduce_fusion.2
  141.9 0.1 reshape.135
  142.1 1.1 bitcast_reduce_fusion.1
  143.2 0.7 gather_fusion.1
  143.9 0.7 gather_fusion.2
  144.7 9.3 %all-to-all-done.4 = bf16[64,2,768]{2,1,0:T(2,128)(2,1)S(1)} async-done(((bf16[64,2,768]{2,1,0:T(2,128)(2,1)}), bf16[64,2,768]{2,1,0:T(2,128)(2,1)S(1)}, u32[]{:S(2)}, u32[]{:S(2)}) %all-to-all-start.4) | async-done | bytes 196640 | tf_op jit(solution)/shard_map/all_to_all | solution.py:32
  153.9 0.1 reshape.137
  154.1 1.1 bitcast_reduce_fusion
  155.2 0.7 gather_fusion.3
  156.0 1.4 bitcast_select_fusion
  157.4 24.9 %all_to_all.90 = bf16[128,128,12]{0,2,1:T(8,128)(2,1)S(1)} all-to-all(bf16[128,128,12]{0,2,1:T(8,128)(2,1)S(1)} %get-tuple-element.30), channel_id=1, replica_groups=mesh['dp'=16,'expert'=64] {'expert'}, dimensions={1} | all-to-all | bytes 786432 | tf_op jit(solution)/shard_map/all_to_all | solution.py:38
  182.3 24.2 %all_to_all.91 = bf16[128,128,12]{0,2,1:T(8,128)(2,1)S(1)} all-to-all(bf16[128,128,12]{0,2,1:T(8,128)(2,1)S(1)} %get-tuple-element.29), channel_id=1, replica_groups=mesh['dp'=16,'expert'=64] {'expert'}, dimensions={1} | all-to-all | bytes 786432 | tf_op jit(solution)/shard_map/all_to_all | solution.py:39
  206.5 5.3 %all-to-all-start.5 = ((bf16[128,128,12]{0,2,1:T(8,128)(2,1)}), bf16[128,128,12]{0,2,1:T(8,128)(2,1)S(1)}, u32[]{:S(2)}, u32[]{:S(2)}) async-start(bf16[128,128,12]{0,2,1:T(8,128)(2,1)} %get-tuple-element.28), calls=%async_computation.5 | async-start | bytes 1048576 | tf_op jit(solution)/shard_map/all_to_all | solution.py:40
  211.8 0.3 copy.43
  212.1 1.1 copy.48
  213.2 0.3 copy.45
  213.5 1.1 copy.49
  214.6 15.8 %all-to-all-done.5 = bf16[128,128,12]{0,2,1:T(8,128)(2,1)S(1)} async-done(((bf16[128,128,12]{0,2,1:T(8,128)(2,1)}), bf16[128,128,12]{0,2,1:T(8,128)(2,1)S(1)}, u32[]{:S(2)}, u32[]{:S(2)}) %all-to-all-start.5) | async-done | bytes 393248 | tf_op jit(solution)/shard_map/all_to_all | solution.py:40
  230.4 0.3 copy.47
  230.7 1.1 copy.50
  (8 shorter events, 0.2 us)
Async XLA Ops:
  7.2 1.2 copy-start
  7.2 79.5 %reduce-scatter.4.cloned.1.call-start = ((), (), s32[]{:S(2)}) async-start(), calls=%async_computation.7 | async-start | bytes 3342336
  16.8 0.9 copy-start.2
  16.8 1.1 copy-start.3
  16.8 1.3 copy-start.4
  17.8 86.6 %copy-start.5 = (s32[128]{0:T(128)S(1)}, s32[128]{0:T(128)}, u32[]{:S(2)}) copy-start(s32[128]{0:T(128)} %constant.129) | copy-start | bytes 1540
  17.8 86.6 %copy-start.1 = (s32[64]{0:T(128)S(1)}, s32[64]{0:T(128)}, u32[]{:S(2)}) copy-start(s32[64]{0:T(128)} %param.21) | copy-start | bytes 772
  17.8 87.9 %copy-start.6 = (s32[128]{0:T(128)S(1)}, s32[128]{0:T(128)}, u32[]{:S(2)}) copy-start(s32[128]{0:T(128)} %param.20) | copy-start | bytes 1540
  17.8 87.9 %copy-start.7 = (s32[64]{0:T(128)S(1)}, s32[64]{0:T(128)}, u32[]{:S(2)}) copy-start(s32[64]{0:T(128)} %param.19) | copy-start | bytes 772
  91.6 24.5 %all-to-all-start = ((bf16[64,2,768]{2,1,0:T(2,128)(2,1)}), bf16[64,2,768]{2,1,0:T(2,128)(2,1)S(1)}, u32[]{:S(2)}, u32[]{:S(2)}) async-start(bf16[64,2,768]{2,1,0:T(2,128)(2,1)} %reshape.132), calls=%async_computation | async-start | bytes 393216 | tf_op jit(solution)/shard_map/all_to_all | solution.py:30
  116.1 18.5 %all-to-all-start.2 = ((bf16[64,2,768]{2,1,0:T(2,128)(2,1)}), bf16[64,2,768]{2,1,0:T(2,128)(2,1)S(1)}, u32[]{:S(2)}, u32[]{:S(2)}) async-start(bf16[64,2,768]{2,1,0:T(2,128)(2,1)} %reshape.134), calls=%async_computation.2 | async-start | bytes 393216 | tf_op jit(solution)/shard_map/all_to_all | solution.py:31
  134.6 19.3 %all-to-all-start.4 = ((bf16[64,2,768]{2,1,0:T(2,128)(2,1)}), bf16[64,2,768]{2,1,0:T(2,128)(2,1)S(1)}, u32[]{:S(2)}, u32[]{:S(2)}) async-start(bf16[64,2,768]{2,1,0:T(2,128)(2,1)} %reshape.136), calls=%async_computation.4 | async-start | bytes 393216 | tf_op jit(solution)/shard_map/all_to_all | solution.py:32
  206.5 23.9 %all-to-all-start.5 = ((bf16[128,128,12]{0,2,1:T(8,128)(2,1)}), bf16[128,128,12]{0,2,1:T(8,128)(2,1)S(1)}, u32[]{:S(2)}, u32[]{:S(2)}) async-start(bf16[128,128,12]{0,2,1:T(8,128)(2,1)} %get-tuple-element.28), calls=%async_computation.5 | async-start | bytes 1048576 | tf_op jit(solution)/shard_map/all_to_all | solution.py:40
Sparse Core Ops, SparseCore 0:
  17.0 69.6 reduce-scatter.3
where the time goes:
time: 239 us
  waiting for transfers between devices  111 us (46%)
  blocking collectives  49.1 us (21%)
  starting transfers between devices  29.9 us (13%)
  local copies, waits for them, and re-layouts  22.8 us (10%)
  between operations  15 us (6%)
  other arithmetic  7.45 us (3%)
  matrix products  3.79 us (2%)
    unnamed x2, waiting for transfers between devices  68.3 us
    all_to_all x1, blocking collectives, collect(): lax.all_to_all(state[0], 'expert', split_axis=1, concat_axis=2, tiled=True)  24.9 us
    all_to_all x1, blocking collectives, collect(): lax.all_to_all(state[1], 'expert', split_axis=1, concat_axis=2, tiled=True)  24.2 us
    all_to_all x1, waiting for transfers between devices, collect(): lax.all_to_all(state[2], 'expert', split_axis=1, concat_axis=2, tiled=True)  15.8 us
    unnamed x31, local copies, waits for them, and re-layouts  14.1 us
    all_to_all x1, starting transfers between devices, spread(): lax.all_to_all(state[0], 'expert', split_axis=2, concat_axis=1, tiled=True)  12.8 us
    all_to_all x1, waiting for transfers between devices, spread(): lax.all_to_all(state[1], 'expert', split_axis=2, concat_axis=1, tiled=True)  9.74 us
    all_to_all x1, waiting for transfers between devices, spread(): lax.all_to_all(state[2], 'expert', split_axis=2, concat_axis=1, tiled=True)  9.26 us
  transfers between devices with their start and end apart: 5, of which 5 were waited for; matrix products, arithmetic and copies ran while one was open for 6% of the time, Pallas kernels for 0%

commit v1 on v0

v1 whole, which is shorter than its diff:
```python
import functools
import math

import jax
import jax.numpy as jnp
from jax import lax
from jax.experimental import pallas as pl
from jax.experimental.pallas import tpu as pltpu
from jax.sharding import PartitionSpec as P

MESH = pl.DeviceIdType.MESH
f32, bf16 = jnp.float32, jnp.bfloat16

beta_one = 0.9
beta_two = 0.95
learn_rate = 0.05
decay_rate = 0.1
epsilon = 1e-08
correct_one = 0.9999734386011124
correct_two = 0.994079470779666


def adamw_step(gradient, weight, first, second):
    first_new = beta_one * first + (1.0 - beta_one) * gradient
    second_new = beta_two * second + (1.0 - beta_two) * gradient * gradient
    direction = first_new / correct_one / (jnp.sqrt(second_new / correct_two) + epsilon)
    weight_new = weight - learn_rate * (direction + decay_rate * weight)
    return weight_new, first_new, second_new


def kernel(
    n_z, n_x, n_y, halves,
    count_ref, table_ref, inputs_ref, cotangent_ref, weights_ref, first_ref, second_ref,
    out_ref,
    masked, masked_other, inputs_other, away, toward, state, state_all, grad, grad_all, updated, chosen,
    pair_send, pair_recv, away_send, away_recv, toward_send, toward_recv,
    state_send, state_recv, grad_send, grad_recv, out_send, out_recv, own_sem,
):
    dp, me = lax.axis_index("dp"), lax.axis_index("expert")
    z, core = dp // 2, dp % 2
    col, row = me // n_y, me % n_y
    experts = n_x * n_y
    long, short = n_z // 2, n_z // 2 - 1
    sign = 1 - 2 * core
    other = z * 2 + 1 - core
    width = cotangent_ref.shape[1] // halves
    share = weights_ref.shape[0]

    def along_z(step):
        return lax.rem(z + step + 2 * n_z, n_z)

    def at_z(step):
        return along_z(step) * 2 + core

    def partner(offset):
        return lax.rem(col + offset // n_y, n_x) * n_y + lax.rem(row + offset % n_y, n_y)

    order = []
    for step in range(long):
        order.append((-(long - step), "away", step))
        if step < short:
            order.append((short - step, "toward", step))
    order.append((0, "own", 0))

    live_rows = lax.broadcasted_iota(jnp.int32, cotangent_ref.shape, 0) < count_ref[0]
    masked[...] = jnp.where(live_rows, cotangent_ref[...], jnp.zeros(cotangent_ref.shape, bf16))
    state[:, 0] = weights_ref[...].reshape(state.shape[0], 2, -1)
    state[:, 1] = first_ref[...].reshape(state.shape[0], 2, -1)
    state[:, 2] = second_ref[...].reshape(state.shape[0], 2, -1)

    barrier = pltpu.get_barrier_semaphore()
    pl.semaphore_signal(barrier, inc=1, device_id=(other, me), device_id_type=MESH)
    pl.semaphore_signal(barrier, inc=1, device_id=(at_z(1), me), device_id_type=MESH)
    pl.semaphore_signal(barrier, inc=1, device_id=(at_z(-1), me), device_id_type=MESH)

    @pl.loop(1, experts)
    def _(offset):
        pl.semaphore_signal(barrier, inc=1, device_id=(dp, partner(offset)), device_id_type=MESH)

    pl.semaphore_wait(barrier, experts + 2)

    def columns_of(step, parity):
        return pl.ds(pl.multiple_of((along_z(step) * 2 + parity) * share, share), share)

    pair = [
        pltpu.make_async_remote_copy(
            masked, masked_other, pair_send.at[len(order)], pair_recv.at[len(order)],
            device_id=(other, me), device_id_type=MESH,
        )
    ]
    for k, (step, _, _) in enumerate(order):
        pair.append(
            pltpu.make_async_remote_copy(
                inputs_ref.at[:, columns_of(-sign * step, 1 - core)], inputs_other.at[k],
                pair_send.at[k], pair_recv.at[k], device_id=(other, me), device_id_type=MESH,
            )
        )
    for copy in pair:
        copy.start()

    @pl.loop(1, experts)
    def _(offset):
        to = partner(offset)
        pltpu.make_async_remote_copy(
            state.at[to], state_all.at[me], state_send, state_recv, device_id=(dp, to), device_id_type=MESH
        ).start()

    own_state = pltpu.make_async_copy(state.at[me], state_all.at[me], own_sem.at[0])
    own_state.start()

    def product(k, half):
        cols = slice(half * width, (half + 1) * width)
        dims = (((0,), (0,)), ((), ()))
        mine = inputs_ref[:, columns_of(sign * order[k][0], core)]
        return lax.dot_general(mine, masked[:, cols], dims, preferred_element_type=f32) + lax.dot_general(
            inputs_other[k], masked_other[:, cols], dims, preferred_element_type=f32
        )

    def hop(buffers, sends, recvs, step, half, to):
        return pltpu.make_async_remote_copy(
            buffers.at[0, step, half], buffers.at[1, step, half], sends.at[step, half], recvs.at[step, half],
            device_id=(to, me), device_id_type=MESH,
        )

    hops = {"away": (away, away_send, away_recv, at_z(-sign)), "toward": (toward, toward_send, toward_recv, at_z(sign))}
    copies = {}
    pair[0].wait_recv()
    for k, (_, way, step) in enumerate(order):
        pair[k + 1].wait_recv()
        for half in range(halves):
            total = product(k, half)
            if way == "own":
                sources = [("away", long - 1)] + ([("toward", short - 1)] if short else [])
            else:
                sources = [(way, step - 1)] if step else []
            for name, before in sources:
                copies[name, before, half].wait_recv()
                total += hops[name][0][1, before, half].astype(f32)
            if way == "own":
                grad[:, :, half * width : (half + 1) * width] = total.astype(bf16).reshape(experts, 2, width)
            else:
                buffers, sends, recvs, to = hops[way]
                buffers[0, step, half] = total.astype(bf16)
                copies[way, step, half] = hop(buffers, sends, recvs, step, half, to)
                copies[way, step, half].start()

    @pl.loop(1, experts)
    def _(offset):
        to = partner(offset)
        pltpu.make_async_remote_copy(
            grad.at[to], grad_all.at[me], grad_send, grad_recv, device_id=(dp, to), device_id_type=MESH
        ).start()

    own_grad = pltpu.make_async_copy(grad.at[me], grad_all.at[me], own_sem.at[1])
    own_grad.start()

    def wait_all(ref, sem):
        part = ref.at[pl.ds(0, experts - 1)]
        pltpu.make_async_copy(part, part, sem).wait()

    own_state.wait()
    wait_all(state_all, state_recv)
    own_grad.wait()
    wait_all(grad_all, grad_recv)

    @pl.loop(0, experts, unroll=4)
    def _(e):
        new = adamw_step(
            grad_all[e].astype(f32),
            state_all[e, 0].astype(f32),
            state_all[e, 1].astype(f32),
            state_all[e, 2].astype(f32),
        )
        for a in range(3):
            updated[e, a] = new[a]

    def choose(to):
        picked = []
        for slot in range(2):
            source = table_ref[2 * to + slot]
            values = updated[jnp.maximum(source, 0)]
            picked.append(jnp.where(source >= 0, values, jnp.zeros_like(values)))
        for a in range(3):
            for r in range(2):
                pairs = [p[a, r : r + 1] for p in picked]
                chosen[to, a, r] = jnp.concatenate(pairs, axis=0).astype(bf16)

    mine = out_ref.at[:, pl.ds(me * 2, 2)]

    @pl.loop(1, experts)
    def _(offset):
        to = partner(offset)
        choose(to)
        pltpu.make_async_remote_copy(
            chosen.at[to], mine, out_send, out_recv, device_id=(dp, to), device_id_type=MESH
        ).start()

    choose(me)
    own_out = pltpu.make_async_copy(chosen.at[me], mine, own_sem.at[2])
    own_out.start()

    for copy in pair:
        copy.wait_send()
    for copy in copies.values():
        copy.wait_send()
    wait_all(state, state_send)
    wait_all(grad, grad_send)
    wait_all(chosen, out_send)
    own_out.wait()
    landed = out_ref.at[:, pl.ds(0, 2 * (experts - 1))]
    pltpu.make_async_copy(landed, landed, out_recv).wait()


def shards(
    n_dp, n_experts,
    expert_inputs, up_cotangent, row_counts, weights, first_moment, second_moment, old_expert, new_expert, slot_counts,
):
    inputs, cotangent = expert_inputs[0, 0], up_cotangent[0, 0]
    n_z = n_dp // 2
    n_x = n_y = math.isqrt(n_experts)
    rows, ff = cotangent.shape
    share = weights.shape[0]
    halves = 2
    long, short = n_z // 2, max(n_z // 2 - 1, 1)

    matches = old_expert[None, :] == new_expert[:, None]
    positions = jnp.arange(n_experts, dtype=jnp.int32)
    source = jnp.sum(jnp.where(matches, positions[None, :], 0), axis=1)
    keep = (jnp.arange(2, dtype=jnp.int32)[None, :] < slot_counts[:, None]).reshape(-1)
    table = jnp.where(keep, source, -1)

    vmem = pl.BlockSpec(memory_space=pltpu.VMEM)
    smem = pl.BlockSpec(memory_space=pltpu.SMEM)
    dma = pltpu.SemaphoreType.DMA
    out = pl.pallas_call(
        functools.partial(kernel, n_z, n_x, n_y, halves),
        out_shape=jax.ShapeDtypeStruct((3, share, 2, ff), bf16),
        in_specs=[smem, smem, vmem, vmem, vmem, vmem, vmem],
        out_specs=pl.BlockSpec(memory_space=pl.ANY),
        scratch_shapes=[
            pltpu.VMEM((rows, ff), bf16),
            pltpu.VMEM((rows, ff), bf16),
            pltpu.VMEM((n_z, rows, share), bf16),
            pltpu.VMEM((2, long, halves, share, ff // halves), bf16),
            pltpu.VMEM((2, short, halves, share, ff // halves), bf16),
            pltpu.VMEM((n_experts, 3, 2, ff), bf16),
            pltpu.VMEM((n_experts, 3, 2, ff), bf16),
            pltpu.VMEM((n_experts, 2, ff), bf16),
            pltpu.VMEM((n_experts, 2, ff), bf16),
            pltpu.VMEM((n_experts, 3, 2, ff), f32),
            pltpu.VMEM((n_experts, 3, 2, 2, ff), bf16),
            dma((n_z + 1,)), dma((n_z + 1,)),
            dma((long, halves)), dma((long, halves)),
            dma((short, halves)), dma((short, halves)),
            dma, dma, dma, dma, dma, dma,
            dma((3,)),
        ],
        compiler_params=pltpu.CompilerParams(collective_id=0, has_side_effects=True, vmem_limit_bytes=32 << 20),
        name="reduce_update_place",
    )(
        row_counts[0], table, inputs, cotangent,
        weights[:, 0], first_moment[:, 0], second_moment[:, 0],
    )
    return out[0], out[1], out[2]


def solution(mesh):
    return jax.shard_map(
        functools.partial(shards, mesh.shape["dp"], mesh.shape["expert"]),
        mesh=mesh,
        in_specs=(
            P("dp", "expert", None, None),
            P("dp", "expert", None, None),
            P("dp", "expert"),
            P("dp", "expert", None),
            P("dp", "expert", None),
            P("dp", "expert", None),
            P(),
            P(),
            P(),
        ),
        out_specs=(P("dp", "expert", None), P("dp", "expert", None), P("dp", "expert", None)),
        check_vma=False,
    )
```

time: 239 us -> 107 us (0.45)
  the two profiles are of different devices: /device:TPU:260 before, /device:TPU:128 now
where the time goes in v1:
time: 107 us; the launch traced here: 106 us
  Pallas kernels  96.8 us (90%)
  local copies, waits for them, and re-layouts  6.79 us (6%)
  other arithmetic  1.5 us (1%)
  between operations  1.31 us (1%)
    pallas_call x1, Pallas kernels, shards(): pl.pallas_call(functools.partial(kernel, n_z, n_x, n_y, halves), out_shap...  96.8 us
    unnamed x10, local copies, waits for them, and re-layouts  4.96 us

profile of v1, /device:TPU:128, one launch (start us, length us, event | category | flops | bytes accessed | tf_op | source)
XLA Modules:
  0.0 106.4 jit_solution(2106206203924209200)
XLA Ops:
  1.3 0.8 select_reduce_fusion
  2.0 0.7 iota_compare_fusion
  2.8 0.1 lt.20
  2.9 0.0 copy-start
  2.9 1.2 %copy-done = bf16[1,1,240,2048]{3,2,1,0:T(8,128)(2,1)S(1)} copy-done((bf16[1,1,240,2048]{3,2,1,0:T(8,128)(2,1)S(1)}, bf16[1,1,240,2048]{3,2,1,0:T(8,128)(2,1)}, u32[]{:S(2)}) %copy-start) | copy-done | bytes 983064
  4.1 0.0 copy-start.1
  4.1 1.0 copy-done.1
  5.1 0.0 copy-start.2
  5.1 0.9 copy-done.2
  6.1 0.0 copy-start.3
  6.1 0.9 copy-done.3
  7.0 0.0 copy-start.4
  7.0 0.9 copy-done.4
  7.9 96.8 %reduce_update_place.1 = bf16[3,128,2,768]{3,2,1,0:T(2,128)(2,1)S(1)} custom-call(s32[1]{0:T(128)} %bitcast.12.count_ref, s32[128]{0:T(128)S(1)} %broadcast_select_fusion.table_ref, bf16[240,2048]{1,0:T(8,128)(2,1)S(1)} %bitcast.13, bf16[240,768]{1,0:T(8,128)(2,1)S(1)} %bitcast.14, bf16[128,768]{1,0:T(8,128)(2,1)S(1)} %bitcast.15, ...), custom_call_target="tpu_custom_call" | custom-call | tf_op jit(solution)/shard_map/reduce_update_place/pallas_call | solution.py:235
  104.7 1.7 %slice_bitcast_fusion = (bf16[128,2,768]{2,1,0:T(2,128)(2,1)}, bf16[128,2,768]{2,1,0:T(2,128)(2,1)}, bf16[128,2,768]{2,1,0:T(2,128)(2,1)}) fusion(bf16[3,128,2,768]{3,2,1,0:T(2,128)(2,1)S(1)} %reduce_update_place.1), kind=kLoop, calls=%fused_computation | loop fusion | bytes 2359296 | tf_op jit(solution)/shard_map/squeeze | solution.py:264
  (1 shorter events, 0.0 us)
Async XLA Ops:
  2.9 1.2 %copy-start = (bf16[1,1,240,2048]{3,2,1,0:T(8,128)(2,1)S(1)}, bf16[1,1,240,2048]{3,2,1,0:T(8,128)(2,1)}, u32[]{:S(2)}) copy-start(bf16[1,1,240,2048]{3,2,1,0:T(8,128)(2,1)} %param.9) | copy-start | bytes 2949124
  4.1 1.0 copy-start.1
  5.1 0.9 copy-start.2
  6.1 0.9 copy-start.3
  7.0 0.9 copy-start.4

commit v2 on v1

v2 whole, which is shorter than its diff:
```python
import functools
import math

import jax
import jax.numpy as jnp
from jax import lax
from jax.experimental import pallas as pl
from jax.experimental.pallas import tpu as pltpu
from jax.sharding import PartitionSpec as P

MESH = pl.DeviceIdType.MESH
f32, bf16 = jnp.float32, jnp.bfloat16

beta_one = 0.9
beta_two = 0.95
learn_rate = 0.05
decay_rate = 0.1
epsilon = 1e-08
correct_one = 0.9999734386011124
correct_two = 0.994079470779666


def adamw_step(gradient, weight, first, second):
    first_new = beta_one * first + (1.0 - beta_one) * gradient
    second_new = beta_two * second + (1.0 - beta_two) * gradient * gradient
    scaled = second_new * (1.0 / correct_two)
    root = scaled * lax.rsqrt(scaled)
    weight_new = (1.0 - learn_rate * decay_rate) * weight - (learn_rate / correct_one) * first_new / (root + epsilon)
    return weight_new, first_new, second_new


def kernel(
    n_z, n_x, n_y, widths, lag,
    count_ref, old_ref, live_ref, new_ref, inputs_ref, cotangent_ref, weights_ref, first_ref, second_ref,
    out_ref,
    inputs, cotangent, moments, names, places, table,
    masked, masked_other, inputs_other, away, toward, state, state_all, grad, grad_all, updated, chosen, relay,
    load_sem, pair_send, pair_recv, away_send, away_recv, toward_send, toward_recv,
    state_send, state_recv, grad_send, grad_recv, out_send, out_recv, own_sem, relay_send, relay_recv,
):
    dp, me = lax.axis_index("dp"), lax.axis_index("expert")
    z, core = dp // 2, dp % 2
    col, row = me // n_y, me % n_y
    experts = n_x * n_y
    long, short = n_z // 2, n_z // 2 - 1
    sign = 1 - 2 * core
    other = z * 2 + 1 - core
    parts = len(widths)
    starts = [sum(widths[:part]) for part in range(parts)]
    share = weights_ref.shape[0]

    def along_z(step):
        return lax.rem(z + step + 2 * n_z, n_z)

    def at_z(step):
        return along_z(step) * 2 + core

    def at(dx, dy):
        return lax.rem(col + dx + n_x, n_x) * n_y + lax.rem(row + dy + n_y, n_y)

    def steps_of(offset):
        offset = lax.rem(offset * 27, experts)
        return offset // n_y, offset % n_y

    def partner(offset):
        return at(*steps_of(offset))

    half_x, half_y = n_x // 2, n_y // 2

    def is_direct(offset):
        dx, dy = steps_of(offset)
        return jnp.logical_not(RELAY & (((dx == half_x) & (dy < half_y)) | ((dy == half_y) & (dx < half_x))))

    def relays():
        for j in range(half_y):
            yield 0, j, at(half_x, j), at(-(half_x // 2), 0), at(-(half_x // 2), j), at(half_x // 2, 0)
        for j in range(half_x):
            yield 1, j, at(j, half_y), at(0, -(half_y // 2)), at(j, -(half_y // 2)), at(0, half_y // 2)

    def used(ref, part):
        here = ref.at[part]
        return here.at[(slice(None),) * (len(here.shape) - 1) + (pl.ds(0, widths[part]),)]

    barrier = pltpu.get_barrier_semaphore()
    pl.semaphore_signal(barrier, inc=1, device_id=(other, me), device_id_type=MESH)
    pl.semaphore_signal(barrier, inc=1, device_id=(at_z(1), me), device_id_type=MESH)
    pl.semaphore_signal(barrier, inc=1, device_id=(at_z(-1), me), device_id_type=MESH)

    @pl.loop(1, experts)
    def _(offset):
        pl.semaphore_signal(barrier, inc=1, device_id=(dp, partner(offset)), device_id_type=MESH)

    loads = [
        pltpu.make_async_copy(source, target, load_sem.at[i])
        for i, (source, target) in enumerate(
            [
                (cotangent_ref, cotangent),
                (inputs_ref, inputs),
                (new_ref, names),
                (weights_ref, moments.at[0]),
                (first_ref, moments.at[1]),
                (second_ref, moments.at[2]),
            ]
        )
    ]
    for copy in loads:
        copy.start()

    order = []
    for step in range(long):
        order.append((-(long - step), "away", step))
        if step < short:
            order.append((short - step, "toward", step))
    order.append((0, "own", 0))

    loads[0].wait()
    live_rows = lax.broadcasted_iota(jnp.int32, cotangent.shape, 0) < count_ref[0]
    masked[...] = jnp.where(live_rows, cotangent[...], jnp.zeros(cotangent.shape, bf16))
    loads[1].wait()
    pl.semaphore_wait(barrier, experts + 2)

    def columns_of(step, parity):
        return pl.ds(pl.multiple_of((along_z(step) * 2 + parity) * share, share), share)

    masks = []
    for part in range(parts):
        cols = slice(starts[part], starts[part] + widths[part])
        masks.append(
            pltpu.make_async_remote_copy(
                masked.at[:, cols], masked_other.at[:, cols],
                pair_send.at[len(order) + part], pair_recv.at[len(order) + part],
                device_id=(other, me), device_id_type=MESH,
            )
        )
    pair = list(masks)
    for k, (step, _, _) in enumerate(order):
        pair.append(
            pltpu.make_async_remote_copy(
                inputs.at[:, columns_of(-sign * step, 1 - core)], inputs_other.at[k],
                pair_send.at[k], pair_recv.at[k], device_id=(other, me), device_id_type=MESH,
            )
        )
    starting = [pair[0], pair[parts], pair[parts + 1], *pair[1:parts], *pair[parts + 2 :]]
    for copy in starting:
        copy.start()

    loads[2].wait()
    slots = lax.broadcasted_iota(jnp.int32, names.shape, 1)

    def place(e, carry):
        found, dead = carry
        found = jnp.where(names[...] == old_ref[e], e, found)
        dead = jnp.where((slots >= 2 * e + live_ref[e]) & (slots < 2 * e + 2), 1, dead)
        return found, dead

    zeros = jnp.zeros(names.shape, jnp.int32)
    found, dead = lax.fori_loop(0, experts, place, (zeros, zeros))
    places[...] = jnp.where(dead == 1, -1, found)
    to_scalars = pltpu.make_async_copy(places, table, load_sem.at[6])
    to_scalars.start()

    for a in range(3):
        loads[3 + a].wait()
        state[:, a] = moments[a].reshape(experts, 2, -1)

    def send_state(first, last):
        @pl.loop(first, last)
        def _(offset):
            to = partner(offset)
            pltpu.make_async_remote_copy(
                state.at[to], state_all.at[me], state_send, state_recv, device_id=(dp, to), device_id_type=MESH
            ).start()

    own_state = pltpu.make_async_copy(state.at[me], state_all.at[me], own_sem.at[2 * parts])
    own_state.start()

    def product(k, part):
        cols = slice(starts[part], starts[part] + widths[part])
        dims = (((0,), (0,)), ((), ()))
        mine = inputs[:, columns_of(sign * order[k][0], core)]
        return lax.dot_general(mine, masked[:, cols], dims, preferred_element_type=f32) + lax.dot_general(
            inputs_other[k], masked_other[:, cols], dims, preferred_element_type=f32
        )

    hops = {"away": (away, away_send, away_recv, at_z(-sign)), "toward": (toward, toward_send, toward_recv, at_z(sign))}
    copies = {}

    def reduce(k, part):
        _, way, step = order[k]
        total = product(k, part)
        if way == "own":
            sources = [("away", long - 1)] + ([("toward", short - 1)] if short else [])
        else:
            sources = [(way, step - 1)] if step else []
        for name, before in sources:
            copies[name, before, part].wait_recv()
            total += hops[name][0][1, before, part, :, : widths[part]].astype(f32)
        if way == "own":
            grad[part, :, :, : widths[part]] = total.astype(bf16).reshape(experts, 2, widths[part])
            send_grad(part)
        else:
            buffers, sends, recvs, to = hops[way]
            buffers[0, step, part, :, : widths[part]] = total.astype(bf16)
            copies[way, step, part] = pltpu.make_async_remote_copy(
                buffers.at[0, step, part, :, pl.ds(0, widths[part])], buffers.at[1, step, part, :, pl.ds(0, widths[part])],
                sends.at[step, part], recvs.at[step, part],
                device_id=(to, me), device_id_type=MESH,
            )
            copies[way, step, part].start()

    own_copies = []

    def send_grad(part):
        @pl.loop(1, experts)
        def _(offset):
            to = partner(offset)
            pltpu.make_async_remote_copy(
                used(grad, part).at[to], used(grad_all, part).at[me], grad_send.at[part], grad_recv.at[part],
                device_id=(dp, to), device_id_type=MESH,
            ).start()

        own_copies.append(
            pltpu.make_async_copy(used(grad, part).at[me], used(grad_all, part).at[me], own_sem.at[part])
        )
        own_copies[-1].start()

    def wait_all(ref, sem):
        part = ref.at[pl.ds(0, experts - 1)]
        pltpu.make_async_copy(part, part, sem).wait()

    def update(part):
        cols = slice(starts[part], starts[part] + widths[part])
        if part == 0:
            own_state.wait()
            wait_all(state_all, state_recv)
        own_copies[part].wait()
        wait_all(used(grad_all, part), grad_recv.at[part])

        batch = min(8, experts)

        @pl.loop(0, experts // batch)
        def _(i):
            some = pl.ds(i * batch, batch)
            new = adamw_step(
                grad_all[part, some, :, : widths[part]].astype(f32),
                state_all[some, 0, :, cols].astype(f32),
                state_all[some, 1, :, cols].astype(f32),
                state_all[some, 2, :, cols].astype(f32),
            )
            for a in range(3):
                updated[part, some, a, :, : widths[part]] = new[a]

    def choose(part, to):
        picked = []
        for slot in range(2):
            source = table[0, 2 * to + slot]
            values = updated[part, jnp.maximum(source, 0), :, :, : widths[part]]
            picked.append(jnp.where(source >= 0, values, jnp.zeros_like(values)))
        for a in range(3):
            for r in range(2):
                pairs = [p[a, r : r + 1] for p in picked]
                chosen[part, to, a, r, :, : widths[part]] = jnp.concatenate(pairs, axis=0).astype(bf16)

    def landing(part, source=me):
        return out_ref.at[:, pl.ds(source * 2, 2), :, pl.ds(starts[part], widths[part])]

    def relay_chosen(part):
        for axis, j, to, by, _, _ in relays():
            choose(part, to)
            pltpu.make_async_remote_copy(
                used(chosen, part).at[to], used(relay, part).at[axis, j], relay_send.at[part], relay_recv.at[part],
                device_id=(dp, by), device_id_type=MESH,
            ).start()

    def forward_chosen(part):
        here = used(relay, part)
        pltpu.make_async_copy(here, here, relay_recv.at[part]).wait()
        for axis, j, _, _, to, source in relays():
            pltpu.make_async_remote_copy(
                here.at[axis, j], landing(part, source), relay_send.at[part], out_recv.at[part],
                device_id=(dp, to), device_id_type=MESH,
            ).start()

    def send_chosen(part, first, last):
        @pl.loop(first, last)
        def _(offset):
            to = partner(offset)

            @pl.when(is_direct(offset))
            def _():
                choose(part, to)
                pltpu.make_async_remote_copy(
                    used(chosen, part).at[to], landing(part), out_send.at[part], out_recv.at[part],
                    device_id=(dp, to), device_id_type=MESH,
                ).start()

        if last == experts:
            choose(part, me)
            own_copies.append(
                pltpu.make_async_copy(used(chosen, part).at[me], landing(part), own_sem.at[parts + part])
            )
            own_copies[-1].start()

    steps = sorted((k + lag * part, part, k) for part in range(parts) for k in range(len(order)))
    spread = 1
    middle = 1 + experts // EARLY

    def finish(part):
        if part == 0:
            to_scalars.wait()
        update(part)
        if RELAY:
            relay_chosen(part)
        send_chosen(part, 1, middle)

    def finish_rest(part):
        send_chosen(part, middle, experts)
        if RELAY:
            forward_chosen(part)

    for i, (_, part, k) in enumerate(steps):
        if part == 0:
            pair[k + parts].wait_recv()
        if k == 0:
            masks[part].wait_recv()
        if order[k][1] == "own" and part > 0:
            finish(part - 1)
        reduce(k, part)
        if order[k][1] == "own" and part > 0:
            finish_rest(part - 1)
        until = 1 + (experts - 1) * min(i + 1, len(order)) // len(order)
        if until > spread:
            send_state(spread, until)
            spread = until
    finish(parts - 1)
    finish_rest(parts - 1)

    for copy in pair:
        copy.wait_send()
    for copy in copies.values():
        copy.wait_send()
    wait_all(state, state_send)
    direct = experts - 1 - (half_x + half_y if RELAY else 0)
    for part in range(parts):
        wait_all(used(grad, part), grad_send.at[part])
        sent = used(chosen, part).at[pl.ds(0, direct)]
        pltpu.make_async_copy(sent, sent, out_send.at[part]).wait()
        if RELAY:
            here = used(relay, part)
            for _ in range(2):
                pltpu.make_async_copy(here, here, relay_send.at[part]).wait()
        own_copies[parts + part].wait()
        landed = out_ref.at[:, pl.ds(0, 2 * (experts - 1)), :, pl.ds(starts[part], widths[part])]
        pltpu.make_async_copy(landed, landed, out_recv.at[part]).wait()


RELAY = False
SPLIT, LAG, EARLY = (1, 2), 2, 4


def shards(
    n_dp, n_experts,
    expert_inputs, up_cotangent, row_counts, weights, first_moment, second_moment, old_expert, new_expert, slot_counts,
):
    inputs, cotangent = expert_inputs[0, 0], up_cotangent[0, 0]
    n_z = n_dp // 2
    n_x = n_y = math.isqrt(n_experts)
    rows, ff = cotangent.shape
    share = weights.shape[0]
    long, short = n_z // 2, max(n_z // 2 - 1, 1)
    widths = [ff * w // sum(SPLIT) for w in SPLIT]
    parts, width = len(widths), max(widths)

    hbm = pl.BlockSpec(memory_space=pltpu.HBM)
    smem = pl.BlockSpec(memory_space=pltpu.SMEM)
    dma = pltpu.SemaphoreType.DMA
    out = pl.pallas_call(
        functools.partial(kernel, n_z, n_x, n_y, widths, LAG),
        out_shape=jax.ShapeDtypeStruct((3, share, 2, ff), bf16),
        in_specs=[smem] * 3 + [hbm] * 6,
        out_specs=hbm,
        scratch_shapes=[
            pltpu.VMEM(inputs.shape, bf16),
            pltpu.VMEM((rows, ff), bf16),
            pltpu.VMEM((3, share, ff), bf16),
            pltpu.VMEM((1, 2 * n_experts), jnp.int32),
            pltpu.VMEM((1, 2 * n_experts), jnp.int32),
            pltpu.SMEM((1, 2 * n_experts), jnp.int32),
            pltpu.VMEM((rows, ff), bf16),
            pltpu.VMEM((rows, ff), bf16),
            pltpu.VMEM((n_z, rows, share), bf16),
            pltpu.VMEM((2, long, parts, share, width), bf16),
            pltpu.VMEM((2, short, parts, share, width), bf16),
            pltpu.VMEM((n_experts, 3, 2, ff), bf16),
            pltpu.VMEM((n_experts, 3, 2, ff), bf16),
            pltpu.VMEM((parts, n_experts, 2, width), bf16),
            pltpu.VMEM((parts, n_experts, 2, width), bf16),
            pltpu.VMEM((parts, n_experts, 3, 2, width), f32),
            pltpu.VMEM((parts, n_experts, 3, 2, 2, width), bf16),
            pltpu.VMEM((parts, 2, n_x // 2, 3, 2, 2, width), bf16),
            dma((7,)),
            dma((n_z + parts,)), dma((n_z + parts,)),
            dma((long, parts)), dma((long, parts)),
            dma((short, parts)), dma((short, parts)),
            dma, dma,
            dma((parts,)), dma((parts,)), dma((parts,)), dma((parts,)),
            dma((2 * parts + 1,)),
            dma((parts,)), dma((parts,)),
        ],
        compiler_params=pltpu.CompilerParams(collective_id=0, has_side_effects=True, vmem_limit_bytes=56 << 20),
        name="reduce_update_place",
    )(
        row_counts[0], old_expert, slot_counts, new_expert[None], inputs, cotangent,
        weights[:, 0], first_moment[:, 0], second_moment[:, 0],
    )
    return out[0], out[1], out[2]


def solution(mesh):
    return jax.shard_map(
        functools.partial(shards, mesh.shape["dp"], mesh.shape["expert"]),
        mesh=mesh,
        in_specs=(
            P("dp", "expert", None, None),
            P("dp", "expert", None, None),
            P("dp", "expert"),
            P("dp", "expert", None),
            P("dp", "expert", None),
            P("dp", "expert", None),
            P(),
            P(),
            P(),
        ),
        out_specs=(P("dp", "expert", None), P("dp", "expert", None), P("dp", "expert", None)),
        check_vma=False,
    )
```

time: 107 us -> 89.8 us (0.84)
  the two profiles are of different devices: /device:TPU:128 before, /device:TPU:16 now
where the time goes in v2:
time: 89.8 us; the launch traced here: 89.6 us
  Pallas kernels  85.4 us (95%)
  local copies, waits for them, and re-layouts  2.92 us (3%)
  between operations  1.29 us (1%)
    pallas_call x1, Pallas kernels, shards(): pl.pallas_call(functools.partial(kernel, n_z, n_x, n_y, widths, LAG), out...  85.4 us
    squeeze x1, local copies, waits for them, and re-layouts, shards(): return (out[0], out[1], out[2])  2.92 us

profile of v2, /device:TPU:16, one launch (start us, length us, event | category | flops | bytes accessed | tf_op | source)
XLA Modules:
  0.0 89.6 jit_solution(7825860698912384481)
XLA Ops:
  1.3 85.4 %reduce_update_place.1 = bf16[3,128,2,768]{3,2,1,0:T(2,128)(2,1)} custom-call(s32[1]{0:T(128)} %bitcast.13.count_ref, s32[64]{0:T(128)} %old_ref.1, s32[64]{0:T(128)} %live_ref.1, s32[1,128]{1,0:T(1,128)} %bitcast.19, bf16[240,2048]{1,0:T(8,128)(2,1)} %bitcast.14, bf16[240,768]{1,0:T(8,128)(2,1)} %bitcast.15, bf16[128,768]{1,0:T(8,128)(2,1)} %bitcast.16, ...), custom_call_target="tpu_custom_call" | custom-call | tf_op jit(solution)/shard_map/reduce_update_place/pallas_call | solution.py:377
  86.7 2.9 %slice_bitcast_fusion = (bf16[128,2,768]{2,1,0:T(2,128)(2,1)}, bf16[128,2,768]{2,1,0:T(2,128)(2,1)}, bf16[128,2,768]{2,1,0:T(2,128)(2,1)}) fusion(bf16[3,128,2,768]{3,2,1,0:T(2,128)(2,1)} %reduce_update_place.1), kind=kLoop, calls=%fused_computation | loop fusion | bytes 2359296 | tf_op jit(solution)/shard_map/squeeze | solution.py:416

commit v3 on v2

--- a/solution.py
+++ b/solution.py
@@ -34,7 +34,7 @@
     count_ref, old_ref, live_ref, new_ref, inputs_ref, cotangent_ref, weights_ref, first_ref, second_ref,
     out_ref,
     inputs, cotangent, moments, names, places, table,
-    masked, masked_other, inputs_other, away, toward, state, state_all, grad, grad_all, updated, chosen, relay,
+    masked, masked_other, inputs_other, own_terms, away, toward, state, state_all, grad, grad_all, updated, chosen, relay,
     load_sem, pair_send, pair_recv, away_send, away_recv, toward_send, toward_recv,
     state_send, state_recv, grad_send, grad_recv, out_send, out_recv, own_sem, relay_send, relay_recv,
 ):
@@ -117,10 +117,16 @@
     live_rows = lax.broadcasted_iota(jnp.int32, cotangent.shape, 0) < count_ref[0]
     masked[...] = jnp.where(live_rows, cotangent[...], jnp.zeros(cotangent.shape, bf16))
     loads[1].wait()
-    pl.semaphore_wait(barrier, experts + 2)
 
     def columns_of(step, parity):
         return pl.ds(pl.multiple_of((along_z(step) * 2 + parity) * share, share), share)
+
+    dims = (((0,), (0,)), ((), ()))
+    for k, (step, _, _) in enumerate(order):
+        mine = inputs[:, columns_of(sign * step, core)]
+        own_terms[k] = lax.dot_general(mine, masked[...], dims, preferred_element_type=f32)
+    pl.semaphore_wait(barrier, experts + 2)
+
 
     masks = []
     for part in range(parts):
@@ -176,9 +182,7 @@
 
     def product(k, part):
         cols = slice(starts[part], starts[part] + widths[part])
-        dims = (((0,), (0,)), ((), ()))
-        mine = inputs[:, columns_of(sign * order[k][0], core)]
-        return lax.dot_general(mine, masked[:, cols], dims, preferred_element_type=f32) + lax.dot_general(
+        return own_terms[k, :, cols] + lax.dot_general(
             inputs_other[k], masked_other[:, cols], dims, preferred_element_type=f32
         )
 
@@ -354,6 +358,23 @@
         pltpu.make_async_copy(landed, landed, out_recv.at[part]).wait()
 
 
+def split(all_ref, weights_ref, first_ref, second_ref, held, load_sem, store_sem):
+    size = all_ref.shape[1] // 2
+    loads, stores = [], []
+    for i in range(2):
+        rows = pl.ds(i * size, size)
+        for a, ref in enumerate([weights_ref, first_ref, second_ref]):
+            loads.append(pltpu.make_async_copy(all_ref.at[a, rows], held.at[a, rows], load_sem.at[a, i]))
+            stores.append(pltpu.make_async_copy(held.at[a, rows], ref.at[rows], store_sem.at[a, i]))
+    for copy in loads:
+        copy.start()
+    for load, store in zip(loads, stores):
+        load.wait()
+        store.start()
+    for copy in stores:
+        copy.wait()
+
+
 RELAY = False
 SPLIT, LAG, EARLY = (1, 2), 2, 4
 
@@ -389,6 +410,7 @@
             pltpu.VMEM((rows, ff), bf16),
             pltpu.VMEM((rows, ff), bf16),
             pltpu.VMEM((n_z, rows, share), bf16),
+            pltpu.VMEM((n_z, share, ff), f32),
             pltpu.VMEM((2, long, parts, share, width), bf16),
             pltpu.VMEM((2, short, parts, share, width), bf16),
             pltpu.VMEM((n_experts, 3, 2, ff), bf16),
@@ -413,7 +435,16 @@
         row_counts[0], old_expert, slot_counts, new_expert[None], inputs, cotangent,
         weights[:, 0], first_moment[:, 0], second_moment[:, 0],
     )
-    return out[0], out[1], out[2]
+    each = jax.ShapeDtypeStruct((share, 2, ff), bf16)
+    return pl.pallas_call(
+        split,
+        out_shape=(each, each, each),
+        in_specs=[hbm],
+        out_specs=(hbm, hbm, hbm),
+        scratch_shapes=[pltpu.VMEM((3, share, 2, ff), bf16), dma((3, 2)), dma((3, 2))],
+        compiler_params=pltpu.CompilerParams(vmem_limit_bytes=56 << 20),
+        name="split_outputs",
+    )(out)
 
 
 def solution(mesh):

time: 89.8 us -> 88.9 us (0.990)
  local copies, waits for them, and re-layouts: 2.92 us -> 0 us
  Pallas kernels: 85.4 us -> 87.4 us
    squeeze x1 -> x0, local copies, waits for them, and re-layouts: 2.92 us -> none  [shards(): return (out[0], out[1], out[2])]
    pallas_call x0 -> x1, Pallas kernels: none -> 2.13 us  [shards(): pl.pallas_call(split, out_shape=(each, each, each), in_specs=[hbm], out_s...]
where the time goes in v3:
time: 88.9 us; the launch traced here: 88.7 us
  Pallas kernels  87.4 us (98%)
  between operations  1.29 us (1%)
    pallas_call x1, Pallas kernels, shards(): pl.pallas_call(functools.partial(kernel, n_z, n_x, n_y, widths, LAG), out...  85.3 us
    pallas_call x1, Pallas kernels, shards(): pl.pallas_call(split, out_shape=(each, each, each), in_specs=[hbm], out_s...  2.13 us

profile of v3, /device:TPU:16, one launch (start us, length us, event | category | flops | bytes accessed | tf_op | source)
XLA Modules:
  0.0 88.7 jit_solution(5520976625328974520)
XLA Ops:
  1.3 85.3 %reduce_update_place.1.all_ref = bf16[3,128,2,768]{3,2,1,0:T(2,128)(2,1)} custom-call(s32[1]{0:T(128)} %bitcast.7.count_ref, s32[64]{0:T(128)} %old_ref.1, s32[64]{0:T(128)} %live_ref.1, s32[1,128]{1,0:T(1,128)} %bitcast.13, bf16[240,2048]{1,0:T(8,128)(2,1)} %bitcast.8, bf16[240,768]{1,0:T(8,128)(2,1)} %bitcast.9, bf16[128,768]{1,0:T(8,128)(2,1)} %bitcast.10, ...), custom_call_target="tpu_custom_call" | custom-call | tf_op jit(solution)/shard_map/reduce_update_place/pallas_call | solution.py:398
  86.6 2.1 %split_outputs.1 = (bf16[128,2,768]{2,1,0:T(2,128)(2,1)}, bf16[128,2,768]{2,1,0:T(2,128)(2,1)}, bf16[128,2,768]{2,1,0:T(2,128)(2,1)}) custom-call(bf16[3,128,2,768]{3,2,1,0:T(2,128)(2,1)} %reduce_update_place.1.all_ref), custom_call_target="tpu_custom_call" | custom-call | tf_op jit(solution)/shard_map/split_outputs/pallas_call | solution.py:439
